TPU v7x, 128 devices: a whole 4x4x4 slice. The times are simulated.
128 devices in a mesh: group: 4 (over y), dev: 32 (over z, x, core).
Axes of the slice: x: 4, y: 4, z: 4, core: 2. Of those that a mesh axis runs over, the one named last changes fastest.
Arguments:
- particles: float32 [4, 16384, 128], P(None, ('group', 'dev')), may hold values from -0.95 to 0.95
- counts: int32 [16384], P(('group', 'dev')), may hold values from 1 to 128, as said below
- upward: float32 [8, 36, 36], replicated, may hold values from -0.375 to 0.375
- downward: float32 [8, 36, 36], replicated, may hold values from -0.75 to 0.75
- translate: float32 [3, 36, 36, 316], replicated, may hold values from -0.0068359375 to 0.0068359375
- far_send: int32 [128, 128, 16], P(('group', 'dev')), may hold values from -1 to 127, as said below
- mid_send: int32 [128, 128, 4], P(('group', 'dev')), may hold values from -1 to 15, as said below
- top_send: int32 [128, 4, 4], P(('group', 'dev')), may hold values from -1 to 63, as said below
- near_send: int32 [128, 128, 8], P(('group', 'dev')), may hold values from -1 to 127, as said below
- far_lists: int32 [316, 16384], P(None, ('group', 'dev')), may hold values from -1 to 2175, as said below
- mid_lists: int32 [316, 2048], P(None, ('group', 'dev')), may hold values from -1 to 527, as said below
- top_lists: int32 [316, 256], P(None, ('group', 'dev')), may hold values from -1 to 79, as said below
- near_lists: int32 [26, 16384], P(None, ('group', 'dev')), may hold values from 0 to 1151, as said below
Outputs:
- potential: float32 [16384, 128], P(('group', 'dev'))
Inputs may be any that keep to these rules, and one draw needn't show every extreme that they name: `counts`: every draw has leaves with 128 particles. `far_send`: row s, column r holds leaves of device s in its first slots and -1 after them; every device fills all 16 slots towards the next rank (wrapping) and at least half of them towards every rank. `mid_send`: as far_send, with middle-level boxes of the sender and 4 slots. `top_send`: entry (s, h, c) indexes the top-level boxes of the sender's group; filled slots come first; every device fills all 4 slots towards the next group (wrapping) and at least half of them towards every group. `near_send`: as far_send, with 8 slots. `far_lists`: slot j stands for the j-th offset of [-3, 3]^3 without [-1, 1]^3 in lexicographic order; it is -1 exactly where that offset leaves the parents' neighbourhood (floor((parity + offset) / 2) outside [-1, 1] in a coordinate, parities the bits of t mod 8 as x + 2 y + 4 z); other entries index leaf_sources of the owner and never an empty received slot. `mid_lists`: as far_lists, for middle-level boxes and mid_sources. `top_lists`: as far_lists, for top-level boxes and top_sources. `near_lists`: entries index near_sources of the owner and never an empty received slot.
All inputs are finite; a program needn't handle non-finite values.
Results may differ from a plain program's by a relative error of at most 0.0003.
Values sent between devices are 32-bit elements; how exact they have to be, the bound alone decides.
No kernel may reach another device: no remote copies, remote signals or barrier semaphores. Data moves between devices by JAX's collectives and lax.ppermute only.
A program may use at most 128 MiB of HBM per device.

v0:
```python
import math

import jax
import jax.numpy as jnp
import numpy as np
from jax import lax
from jax.sharding import PartitionSpec as P

ORDER = 6


SOFTEN = 0.01


def harmonics(offsets):
    coord_x = offsets[0]
    coord_y = offsets[1]
    coord_z = offsets[2]
    radius_sq = coord_x * coord_x + coord_y * coord_y + coord_z * coord_z
    real_part = {(0, 0): jnp.ones_like(coord_x)}
    imag_part = {(0, 0): jnp.zeros_like(coord_x)}
    for degree in range(1, ORDER):
        prior_re = real_part[degree - 1, degree - 1]
        prior_im = imag_part[degree - 1, degree - 1]
        real_part[degree, degree] = (coord_x * prior_re - coord_y * prior_im) / (2.0 * degree)
        imag_part[degree, degree] = (coord_x * prior_im + coord_y * prior_re) / (2.0 * degree)
        for column in range(degree):
            upper_re = (2.0 * degree - 1.0) * coord_z * real_part[degree - 1, column]
            upper_im = (2.0 * degree - 1.0) * coord_z * imag_part[degree - 1, column]
            if column <= degree - 2:
                upper_re = upper_re - radius_sq * real_part[degree - 2, column]
                upper_im = upper_im - radius_sq * imag_part[degree - 2, column]
            factor = 1.0 / ((degree + column) * (degree - column))
            real_part[degree, column] = upper_re * factor
            imag_part[degree, column] = upper_im * factor
    pieces = []
    for degree in range(ORDER):
        for column in range(degree + 1):
            weight = math.sqrt(math.factorial(degree - column) * math.factorial(degree + column))
            pieces.append(weight * real_part[degree, column])
            if column > 0:
                pieces.append(weight * imag_part[degree, column])
    return jnp.stack(pieces, axis=0)


def near_offsets():
    shifts = []
    for step_x in (-1, 0, 1):
        for step_y in (-1, 0, 1):
            for step_z in (-1, 0, 1):
                if step_x != 0 or step_y != 0 or step_z != 0:
                    shifts.append((step_x, step_y, step_z))
    return np.array(shifts, dtype=np.float32)


def pair_field(targets, sources, displace, exclude):
    diff_x = targets[0][:, :, None] - sources[0][:, None, :] - displace[0]
    diff_y = targets[1][:, :, None] - sources[1][:, None, :] - displace[1]
    diff_z = targets[2][:, :, None] - sources[2][:, None, :] - displace[2]
    inverse = lax.rsqrt(diff_x * diff_x + diff_y * diff_y + diff_z * diff_z + SOFTEN)
    weighted = sources[3][:, None, :] * inverse
    if exclude:
        slot_count = targets.shape[2]
        same_slot = jnp.arange(slot_count)[:, None] == jnp.arange(slot_count)[None, :]
        weighted = jnp.where(same_slot[None], 0.0, weighted)
    return jnp.sum(weighted, axis=2)


def translate_level(operator, source_table, source_lists):
    clipped = jnp.maximum(source_lists, 0)
    picked = jnp.take(source_table, clipped, axis=1)
    picked = jnp.where(source_lists[None] >= 0, picked, 0.0)
    term_count = operator.shape[0]
    return jnp.dot(
        operator.reshape(term_count, -1),
        picked.reshape(-1, source_lists.shape[1]),
        precision=lax.Precision.HIGHEST,
    )


def upward_pass(upward, moments):
    term_count, box_count = moments.shape
    grouped = moments.reshape(term_count, box_count // 8, 8)
    return jnp.einsum("oik,kqo->iq", upward, grouped, precision=lax.Precision.HIGHEST)


def downward_pass(downward, parents, children):
    term_count, box_count = parents.shape
    spread = jnp.einsum("oik,kq->iqo", downward, parents, precision=lax.Precision.HIGHEST)
    return children + spread.reshape(term_count, box_count * 8)


def pick_sends(moments, send_rows):
    picked = jnp.take(moments, jnp.maximum(send_rows, 0), axis=1)
    return jnp.where(send_rows[None] >= 0, picked, 0.0)


def local(
    particles,
    counts,
    upward,
    downward,
    translate,
    far_send,
    mid_send,
    top_send,
    near_send,
    far_lists,
    mid_lists,
    top_lists,
    near_lists,
):
    slot_count = particles.shape[2]
    term_count = upward.shape[1]
    filled = jnp.arange(slot_count)[None, :] < counts[:, None]
    charge = jnp.where(filled, particles[3], 0.0)
    packed = jnp.concatenate([particles[:3], charge[None]], axis=0)
    near_rows = near_send[0]
    near_out = jnp.take(packed, jnp.maximum(near_rows, 0), axis=1)
    near_out = jnp.where(near_rows[None, :, :, None] >= 0, near_out, 0.0)
    basis_values = harmonics(particles[:3])
    leaf_moments = jnp.einsum("kbp,bp->kb", basis_values, charge, precision=lax.Precision.HIGHEST)
    mid_moments = upward_pass(upward, leaf_moments)
    top_moments = upward_pass(upward, mid_moments)
    leaf_out = pick_sends(leaf_moments, far_send[0])
    mid_out = pick_sends(mid_moments, mid_send[0])
    near_in = lax.all_to_all(near_out, ("group", "dev"), split_axis=1, concat_axis=1, tiled=True)
    leaf_in, mid_in = (
        lax.all_to_all(leaf_out, ("group", "dev"), split_axis=1, concat_axis=1, tiled=True),
        lax.all_to_all(mid_out, ("group", "dev"), split_axis=1, concat_axis=1, tiled=True),
    )
    group_table = lax.all_gather(top_moments, "dev", axis=1, tiled=True)
    top_out = pick_sends(group_table, top_send[0])
    top_in = lax.all_to_all(top_out, "group", split_axis=1, concat_axis=1, tiled=True)
    top_table = jnp.concatenate([group_table, top_in.reshape(term_count, -1)], axis=1)
    top_local = translate_level(translate[2], top_table, top_lists)
    near_field = pair_field(packed, packed, (0.0, 0.0, 0.0), True)
    near_table = jnp.concatenate([packed, near_in.reshape(4, -1, slot_count)], axis=1)
    shifts = near_offsets()
    for slot_index in range(shifts.shape[0]):
        sources = jnp.take(near_table, near_lists[slot_index], axis=1)
        displace = tuple((2.0 * float(value) for value in shifts[slot_index]))
        near_field = near_field + pair_field(packed, sources, displace, False)
    leaf_table = jnp.concatenate([leaf_moments, leaf_in.reshape(term_count, -1)], axis=1)
    leaf_local = translate_level(translate[0], leaf_table, far_lists)
    mid_table = jnp.concatenate([mid_moments, mid_in.reshape(term_count, -1)], axis=1)
    mid_local = translate_level(translate[1], mid_table, mid_lists)
    mid_total = downward_pass(downward, top_local, mid_local)
    leaf_total = downward_pass(downward, mid_total, leaf_local)
    far_field = jnp.einsum("kb,kbp->bp", leaf_total, basis_values, precision=lax.Precision.HIGHEST)
    return jnp.where(filled, near_field + far_field, 0.0)


def solution(mesh):
    in_specs = (
        P(None, ("group", "dev"), None),
        P(("group", "dev")),
        P(),
        P(),
        P(),
        P(("group", "dev"), None, None),
        P(("group", "dev"), None, None),
        P(("group", "dev"), None, None),
        P(("group", "dev"), None, None),
        P(None, ("group", "dev")),
        P(None, ("group", "dev")),
        P(None, ("group", "dev")),
        P(None, ("group", "dev")),
    )
    out_specs = P(("group", "dev"), None)
    return jax.shard_map(local, mesh=mesh, in_specs=in_specs, out_specs=out_specs, check_vma=False)
```

profile of v0, /device:TPU:1, one launch (start us, length us, event | category | flops | bytes accessed | tf_op | source)
XLA Modules:
  0.0 526.6 jit_solution(4611583596009665121)
XLA Ops:
  30.0 5.1 fusion.2
  35.5 26.8 %all-gather = f32[32,2,36]{2,1,0:T(2,128)S(1)} all-gather(f32[1,2,36]{2,1,0:T(2,128)S(1)} %convolution_bitcast_fusion.5), channel_id=1, replica_groups=mesh['group'=4,'dev'=32] {'dev'}, dimensions={0}, use_global_device_ids=true | all-gather | bytes 9504 | tf_op jit(solution)/shard_map/all_gather | solution.py:132
  64.1 4.4 all-to-all-start.3
  73.2 5.9 %fusion.17 = (f32[1,36,36,316]{3,2,1,0:T(8,128)}, f32[1,36,36,316]{3,2,1,0:T(8,128)}, f32[1,36,36,316]{3,2,1,0:T(8,128)}) fusion(f32[3,36,36,316]{3,2,1,0:T(8,128)} %param.19), kind=kLoop, calls=%fused_computation.296 | loop fusion | bytes 9828864 | tf_op jit(solution)/shard_map/slice | solution.py:145
  80.4 8.1 %gather_fusion = f32[1024,4,128]{2,1,0:T(4,128)} fusion(f32[4,128,128]{2,0,1:T(4,128)S(1)} %pad_maximum_fusion.3, s32[1024]{0:T(1024)S(1)} %get-tuple-element.275), kind=kCustom, calls=%fused_computation.26 | custom fusion | bytes 4198400 | tf_op jit(solution)/shard_map/jit(_take)/gather | solution.py:119
  95.0 5.5 %gather_fusion.1 = f32[2048,36]{1,0:T(8,128)S(1)} fusion(f32[36,128]{0,1:T(8,128)S(1)} %bitcast.368, s32[2048]{0:T(1024)S(1)} %broadcast_clamp_fusion), kind=kCustom, calls=%fused_computation.27 | custom fusion | bytes 598016 | tf_op jit(solution)/shard_map/jit(_take)/gather | solution.py:94
  101.6 6.8 %select_bitcast_fusion.1 = f32[4,128,8,128]{3,0,2,1:T(4,128)} fusion(f32[128,8,4,128]{3,2,1,0:T(4,128)} %bitcast.377, pred[128,8]{1,0:T(8,128)(4,1)S(1)} %copy.155, pred[128,8]{1,0:T(8,128)(4,1)S(1)} %copy.156), kind=kLoop, calls=%fused_computation.66 | loop fusion | flops 1048576 | bytes 4196352 | tf_op jit(solution)/shard_map/jit(_where)/select_n | solution.py:120
  108.4 2.1 fusion.44
  111.5 2.9 reshape.745
  114.3 3.0 reshape_squeeze.11
  118.3 3.0 reshape_squeeze.10
  123.1 7.6 %all-to-all-start.2 = ((f32[128,1,144]{2,1,0:T(1,128)}), f32[128,1,144]{2,1,0:T(1,128)S(1)}, u32[]{:S(2)}, u32[]{:S(2)}) async-start(f32[128,1,144]{2,1,0:T(1,128)} %reshape.741), calls=%async_computation.2 | async-start | bytes 262144 | tf_op jit(solution)/shard_map/all_to_all | solution.py:130
  135.6 5.1 all-to-all-done.2
  140.6 4.7 all-to-all-start.1
  147.1 13.6 %gather_fusion.4 = f32[5056,36]{1,0:T(8,128)S(1)} fusion(f32[36,528]{0,1:T(8,128)S(1)} %pad_maximum_fusion.2, s32[5120]{0:T(1024)S(1)} %pad_clamp_fusion.1), kind=kCustom, calls=%fused_computation.30 | custom fusion | bytes 1476352 | tf_op jit(solution)/shard_map/jit(_take)/gather | solution.py:71
  162.7 10.2 %all-to-all-start = ((f32[4,128,8,128]{3,0,2,1:T(4,128)}), f32[4,128,8,128]{3,0,2,1:T(4,128)}, u32[]{:S(2)}, u32[]{:S(2)}) async-start(f32[4,128,8,128]{3,0,2,1:T(4,128)} %select_bitcast_fusion.1), calls=%async_computation | async-start | bytes 4194304 | tf_op jit(solution)/shard_map/all_to_all | solution.py:127
  175.4 2.7 fusion.7
  178.9 2.4 reduce.2
  182.0 81.8 %gather_fusion.2 = f32[40448,36]{1,0:T(8,128)} fusion(f32[36,2176]{0,1:T(8,128)S(1)} %pad_maximum_fusion.1, s32[40960]{0:T(1024)} %pad_clamp_fusion), kind=kCustom, calls=%fused_computation.28 | custom fusion | bytes 11810816 | tf_op jit(solution)/shard_map/jit(_take)/gather | solution.py:71
  263.8 14.9 %copy.161 = f32[316,128,36]{1,0,2:T(8,128)} copy(f32[316,128,36]{2,1,0:T(8,128)} %bitcast.371) | data formatting | bytes 11649024 | tf_op jit(solution)/shard_map/jit(_take)/gather | solution.py:71
  278.7 6.2 %select_bitcast_fusion = f32[36,316,128]{2,1,0:T(8,128)} fusion(f32[316,128,36]{1,0,2:T(8,128)} %copy.161, pred[316,128]{1,0:T(8,128)(4,1)S(1)} %copy-done.16, pred[316,128]{1,0:T(8,128)(4,1)S(1)} %copy-done.15), kind=kLoop, calls=%fused_computation.60 | loop fusion | flops 2912256 | bytes 11729920 | tf_op jit(solution)/shard_map/jit(_where)/select_n | solution.py:72
  284.9 6.5 %select_n.165 = f32[11376,128]{1,0:T(8,128)} reshape(f32[36,316,128]{2,1,0:T(8,128)} %select_bitcast_fusion) | data formatting | bytes 11649024 | tf_op jit(solution)/shard_map/jit(_where)/select_n | solution.py:72
  291.4 6.8 %fusion.5 = f32[36,128,1]{1,0,2:T(8,128)S(1)} fusion(f32[36,128]{1,0:T(8,128)S(1)} %copy.177, f32[11376,128]{1,0:T(8,128)} %select_n.165, f32[36,11376]{1,0:T(8,128)} %reshape_squeeze.9), kind=kOutput, calls=%fused_computation.71 | convolution fusion | flops 629051904 | bytes 7499520 | tf_op jit(solution)/shard_map/dot_general | solution.py:74
  298.4 3.4 fusion
  301.9 2.4 pad_maximum_fusion
  356.4 21.1 %multiply_reduce_fusion.2 = (f32[128,128]{1,0:T(8,128)S(1)}, f32[128,128]{1,0:T(8,128)S(1)}, f32[128,128]{1,0:T(8,128)S(1)}) fusion(f32[128,128]{1,0:T(8,128)} %bitcast.479, f32[128,128]{1,0:T(8,128)} %bitcast.480, f32[128,128]{1,0:T(8,128)} %bitcast.481, f32[128,128]{1,0:T(8,128)} %bitcast.478, f32[128,128]{1,0:T(8,128)S(1)} %copy-done.20, ...), kind=kLoop, calls=%fused_computation.35 | loop fusion | flops 85934080 | bytes 1179648 | tf_op jit(solution)/shard_map/reduce_sum | solution.py:66
  377.7 24.9 %select_reduce_fusion = (f32[128,128]{1,0:T(8,128)S(1)}, f32[128,128]{1,0:T(8,128)S(1)}, f32[128,128]{1,0:T(8,128)S(1)}, f32[128,128]{1,0:T(8,128)S(1)}) fusion(f32[128,128]{1,0:T(8,128)S(1)} %copy-done.20, f32[128,128]{1,0:T(8,128)S(1)} %copy-done.19, f32[128,128]{1,0:T(8,128)S(1)} %copy-done.18, f32[128,128]{1,0:T(8,128)S(1)} %copy-done.14, ...), kind=kLoop, calls=%fused_computation.59 | loop fusion | flops 106889216 | bytes 1327104 | tf_op jit(solution)/shard_map/reduce_sum | solution.py:66
  402.8 24.2 %multiply_reduce_fusion.25 = (f32[128,128]{1,0:T(8,128)S(1)}, f32[128,128]{1,0:T(8,128)S(1)}, f32[128,128]{1,0:T(8,128)S(1)}, f32[128,128]{1,0:T(8,128)S(1)}) fusion(f32[128,128]{1,0:T(8,128)S(1)} %bitcast.395, f32[128,128]{1,0:T(8,128)S(1)} %bitcast.396, f32[128,128]{1,0:T(8,128)S(1)} %bitcast.397, f32[128,128]{1,0:T(8,128)S(1)} %bitcast.394, ...), kind=kLoop, calls=%fused_computation.58 | loop fusion | flops 113180672 | bytes 1507328 | tf_op jit(solution)/shard_map/reduce_sum | solution.py:66
  427.4 24.8 %multiply_reduce_fusion.18 = (f32[128,128]{1,0:T(8,128)S(1)}, f32[128,128]{1,0:T(8,128)S(1)}, f32[128,128]{1,0:T(8,128)S(1)}, f32[128,128]{1,0:T(8,128)S(1)}) fusion(f32[128,128]{1,0:T(8,128)S(1)} %bitcast.403, f32[128,128]{1,0:T(8,128)S(1)} %bitcast.404, f32[128,128]{1,0:T(8,128)S(1)} %bitcast.405, f32[128,128]{1,0:T(8,128)S(1)} %bitcast.402, ...), kind=kLoop, calls=%fused_computation.51 | loop fusion | flops 108986368 | bytes 1507328 | tf_op jit(solution)/shard_map/reduce_sum | solution.py:66
  452.5 23.9 %multiply_reduce_fusion.14 = (f32[128,128]{1,0:T(8,128)S(1)}, f32[128,128]{1,0:T(8,128)S(1)}, f32[128,128]{1,0:T(8,128)S(1)}, f32[128,128]{1,0:T(8,128)S(1)}) fusion(f32[128,128]{1,0:T(8,128)S(1)} %bitcast.423, f32[128,128]{1,0:T(8,128)S(1)} %bitcast.424, f32[128,128]{1,0:T(8,128)S(1)} %bitcast.425, f32[128,128]{1,0:T(8,128)S(1)} %bitcast.422, ...), kind=kLoop, calls=%fused_computation.47 | loop fusion | flops 104792064 | bytes 1507328 | tf_op jit(solution)/shard_map/reduce_sum | solution.py:66
  476.8 24.3 %multiply_reduce_fusion.10 = (f32[128,128]{1,0:T(8,128)S(1)}, f32[128,128]{1,0:T(8,128)S(1)}, f32[128,128]{1,0:T(8,128)S(1)}, f32[128,128]{1,0:T(8,128)S(1)}) fusion(f32[128,128]{1,0:T(8,128)S(1)} %bitcast.443, f32[128,128]{1,0:T(8,128)S(1)} %bitcast.444, f32[128,128]{1,0:T(8,128)S(1)} %bitcast.445, f32[128,128]{1,0:T(8,128)S(1)} %bitcast.442, ...), kind=kLoop, calls=%fused_computation.43 | loop fusion | flops 108986368 | bytes 1507328 | tf_op jit(solution)/shard_map/reduce_sum | solution.py:66
  501.2 24.3 %multiply_reduce_fusion.6 = (f32[128,128]{1,0:T(8,128)S(1)}, f32[128,128]{1,0:T(8,128)S(1)}, f32[128,128]{1,0:T(8,128)S(1)}, f32[128,128]{1,0:T(8,128)S(1)}) fusion(f32[128,128]{1,0:T(8,128)S(1)} %bitcast.459, f32[128,128]{1,0:T(8,128)S(1)} %bitcast.460, f32[128,128]{1,0:T(8,128)S(1)} %bitcast.461, f32[128,128]{1,0:T(8,128)S(1)} %bitcast.458, ...), kind=kLoop, calls=%fused_computation.39 | loop fusion | flops 108986368 | bytes 1507328 | tf_op jit(solution)/shard_map/reduce_sum | solution.py:66
  (474 shorter events, 114.3 us)
Async XLA Ops:
  0.0 145.3 %copy-start = (f32[8,36,36]{2,0,1:T(8,128)S(1)}, f32[8,36,36]{2,0,1:T(8,128)}, u32[]{:S(2)}) copy-start(f32[8,36,36]{2,0,1:T(8,128)} %param.18) | copy-start | bytes 124420
  0.0 29.8 %copy-start.2 = (f32[4,128,128]{2,1,0:T(8,128)S(1)}, f32[4,128,128]{2,1,0:T(8,128)}, u32[]{:S(2)}) copy-start(f32[4,128,128]{2,1,0:T(8,128)} %param.15) | copy-start | bytes 786436
  0.0 71.3 %slice-start = ((f32[4,128,128]{2,1,0:T(8,128)}), f32[3,128,128]{2,1,0:T(8,128)S(1)}, s32[]{:S(2)}) async-start(f32[4,128,128]{2,1,0:T(8,128)} %param.15), calls=%async_computation.4 | async-start | bytes 393216 | tf_op jit(solution)/shard_map/slice | solution.py:117
  0.0 35.0 %copy-start.11 = (f32[8,36,36]{2,0,1:T(8,128)S(1)}, f32[8,36,36]{2,0,1:T(8,128)}, u32[]{:S(2)}) copy-start(f32[8,36,36]{2,0,1:T(8,128)} %param.17) | copy-start | bytes 124420
  0.0 62.3 %copy-start.107 = (s32[316,2]{0,1:T(2,128)S(1)}, s32[316,2]{0,1:T(2,128)}, u32[]{:S(2)}) copy-start(s32[316,2]{0,1:T(2,128)} %param.26) | copy-start | bytes 7588
  0.0 68.4 %copy-start.108 = (s32[26,128]{1,0:T(8,128)S(1)}, s32[26,128]{1,0:T(8,128)}, u32[]{:S(2)}) copy-start(s32[26,128]{1,0:T(8,128)} %param.27) | copy-start | bytes 39940
  0.0 69.8 %copy-start.106 = (s32[1,128,8]{1,2,0:T(8,128)S(1)}, s32[1,128,8]{1,2,0:T(8,128)}, u32[]{:S(2)}) copy-start(s32[1,128,8]{1,2,0:T(8,128)} %param.23) | copy-start | bytes 12292
  0.1 70.4 %copy-start.104 = (s32[1,128,16]{1,2,0:T(8,128)S(1)}, s32[1,128,16]{1,2,0:T(8,128)}, u32[]{:S(2)}) copy-start(s32[1,128,16]{1,2,0:T(8,128)} %param.20) | copy-start | bytes 24580
  0.1 70.4 %copy-start.12 = (s32[316,128]{1,0:T(8,128)S(1)}, s32[316,128]{1,0:T(8,128)}, u32[]{:S(2)}) copy-start(s32[316,128]{1,0:T(8,128)} %param.24) | copy-start | bytes 485380
  0.1 71.1 %copy-start.109 = (s32[1,128,4]{1,2,0:T(4,128)S(1)}, s32[1,128,4]{1,2,0:T(4,128)}, u32[]{:S(2)}) copy-start(s32[1,128,4]{1,2,0:T(4,128)} %param.21) | copy-start | bytes 6148
  0.1 71.1 %copy-start.17 = (s32[316,16]{0,1:T(8,128)S(1)}, s32[316,16]{0,1:T(8,128)}, u32[]{:S(2)}) copy-start(s32[316,16]{0,1:T(8,128)} %param.25) | copy-start | bytes 60676
  5.2 57.2 %copy-start.13 = (f32[128,128]{1,0:T(8,128)}, f32[128,128]{1,0:T(8,128)S(1)}, u32[]{:S(2)}) copy-start(f32[128,128]{1,0:T(8,128)S(1)} %bitcast_select_fusion) | copy-start | bytes 196612
  64.1 59.1 %all-to-all-start.3 = ((f32[4,1,144]{2,1,0:T(1,128)}), f32[4,1,144]{2,1,0:T(1,128)S(1)}, u32[]{:S(2)}, u32[]{:S(2)}) async-start(f32[4,1,144]{2,1,0:T(1,128)} %reshape.743), calls=%async_computation.3 | async-start | bytes 8192 | tf_op jit(solution)/shard_map/all_to_all | solution.py:134
  123.1 17.5 %all-to-all-start.2 = ((f32[128,1,144]{2,1,0:T(1,128)}), f32[128,1,144]{2,1,0:T(1,128)S(1)}, u32[]{:S(2)}, u32[]{:S(2)}) async-start(f32[128,1,144]{2,1,0:T(1,128)} %reshape.741), calls=%async_computation.2 | async-start | bytes 262144 | tf_op jit(solution)/shard_map/all_to_all | solution.py:130
  140.6 22.1 %all-to-all-start.1 = ((f32[128,1,576]{2,1,0:T(1,128)}), f32[128,1,576]{2,1,0:T(1,128)S(1)}, u32[]{:S(2)}, u32[]{:S(2)}) async-start(f32[128,1,576]{2,1,0:T(1,128)} %reshape.745), calls=%async_computation.1 | async-start | bytes 655360 | tf_op jit(solution)/shard_map/all_to_all | solution.py:129
  162.7 139.2 %all-to-all-start = ((f32[4,128,8,128]{3,0,2,1:T(4,128)}), f32[4,128,8,128]{3,0,2,1:T(4,128)}, u32[]{:S(2)}, u32[]{:S(2)}) async-start(f32[4,128,8,128]{3,0,2,1:T(4,128)} %select_bitcast_fusion.1), calls=%async_computation | async-start | bytes 4194304 | tf_op jit(solution)/shard_map/all_to_all | solution.py:127
  348.7 28.8 %copy-start.14 = (f32[128,128]{1,0:T(8,128)S(1)}, f32[128,128]{1,0:T(8,128)}, u32[]{:S(2)}) copy-start(f32[128,128]{1,0:T(8,128)} %copy-done.13) | copy-start | bytes 196612
  348.7 28.8 %copy-start.105 = (pred[128,128]{1,0:T(8,128)(4,1)S(1)}, pred[128,128]{1,0:T(8,128)(4,1)}, u32[]{:S(2)}) copy-start(pred[128,128]{1,0:T(8,128)(4,1)} %iota_compare_fusion.1) | copy-start | bytes 49156
  427.0 25.3 %copy-start.48 = (f32[1,128,128]{2,0,1:T(1,128)S(1)}, f32[1,128,128]{2,0,1:T(1,128)}, u32[]{:S(2)}) copy-start(f32[1,128,128]{2,0,1:T(1,128)} %get-tuple-element.158) | copy-start | bytes 196612
  427.1 25.3 %copy-start.49 = (f32[1,128,128]{2,0,1:T(1,128)S(1)}, f32[1,128,128]{2,0,1:T(1,128)}, u32[]{:S(2)}) copy-start(f32[1,128,128]{2,0,1:T(1,128)} %get-tuple-element.159) | copy-start | bytes 196612
  427.1 25.3 %copy-start.50 = (f32[1,128,128]{2,0,1:T(1,128)S(1)}, f32[1,128,128]{2,0,1:T(1,128)}, u32[]{:S(2)}) copy-start(f32[1,128,128]{2,0,1:T(1,128)} %get-tuple-element.160) | copy-start | bytes 196612
  427.1 25.3 %copy-start.51 = (f32[1,128,128]{2,0,1:T(1,128)S(1)}, f32[1,128,128]{2,0,1:T(1,128)}, u32[]{:S(2)}) copy-start(f32[1,128,128]{2,0,1:T(1,128)} %get-tuple-element.161) | copy-start | bytes 196612
  427.1 25.3 %copy-start.60 = (f32[1,128,128]{2,0,1:T(1,128)S(1)}, f32[1,128,128]{2,0,1:T(1,128)}, u32[]{:S(2)}) copy-start(f32[1,128,128]{2,0,1:T(1,128)} %get-tuple-element.154) | copy-start | bytes 196612
  427.1 25.3 %copy-start.61 = (f32[1,128,128]{2,0,1:T(1,128)S(1)}, f32[1,128,128]{2,0,1:T(1,128)}, u32[]{:S(2)}) copy-start(f32[1,128,128]{2,0,1:T(1,128)} %get-tuple-element.155) | copy-start | bytes 196612
  427.1 25.3 %copy-start.62 = (f32[1,128,128]{2,0,1:T(1,128)S(1)}, f32[1,128,128]{2,0,1:T(1,128)}, u32[]{:S(2)}) copy-start(f32[1,128,128]{2,0,1:T(1,128)} %get-tuple-element.156) | copy-start | bytes 196612
  427.1 25.3 %copy-start.63 = (f32[1,128,128]{2,0,1:T(1,128)S(1)}, f32[1,128,128]{2,0,1:T(1,128)}, u32[]{:S(2)}) copy-start(f32[1,128,128]{2,0,1:T(1,128)} %get-tuple-element.157) | copy-start | bytes 196612
  427.1 25.3 %copy-start.64 = (f32[1,128,128]{2,0,1:T(1,128)S(1)}, f32[1,128,128]{2,0,1:T(1,128)}, u32[]{:S(2)}) copy-start(f32[1,128,128]{2,0,1:T(1,128)} %get-tuple-element.150) | copy-start | bytes 196612
  427.1 25.3 %copy-start.65 = (f32[1,128,128]{2,0,1:T(1,128)S(1)}, f32[1,128,128]{2,0,1:T(1,128)}, u32[]{:S(2)}) copy-start(f32[1,128,128]{2,0,1:T(1,128)} %get-tuple-element.151) | copy-start | bytes 196612
  427.1 25.3 %copy-start.66 = (f32[1,128,128]{2,0,1:T(1,128)S(1)}, f32[1,128,128]{2,0,1:T(1,128)}, u32[]{:S(2)}) copy-start(f32[1,128,128]{2,0,1:T(1,128)} %get-tuple-element.152) | copy-start | bytes 196612
  427.2 25.3 %copy-start.67 = (f32[1,128,128]{2,0,1:T(1,128)S(1)}, f32[1,128,128]{2,0,1:T(1,128)}, u32[]{:S(2)}) copy-start(f32[1,128,128]{2,0,1:T(1,128)} %get-tuple-element.153) | copy-start | bytes 196612
  427.2 25.3 %copy-start.72 = (f32[1,128,128]{2,0,1:T(1,128)S(1)}, f32[1,128,128]{2,0,1:T(1,128)}, u32[]{:S(2)}) copy-start(f32[1,128,128]{2,0,1:T(1,128)} %get-tuple-element.146) | copy-start | bytes 196612
  427.2 25.3 %copy-start.73 = (f32[1,128,128]{2,0,1:T(1,128)S(1)}, f32[1,128,128]{2,0,1:T(1,128)}, u32[]{:S(2)}) copy-start(f32[1,128,128]{2,0,1:T(1,128)} %get-tuple-element.147) | copy-start | bytes 196612
  (107 other events, 2351.7 us)
where the time goes:
time: 537 us; the launch traced here: 527 us
  other arithmetic  239 us (45%)
  local copies, waits for them, and re-layouts  204 us (38%)
  starting transfers between devices  26.9 us (5%)
  blocking collectives  26.8 us (5%)
  matrix products  21.3 us (4%)
    reduce_sum x7, other arithmetic, pair_field(): return jnp.sum(weighted, axis=2)  168 us
    gather x6, local copies, waits for them, and re-layouts, translate_level(): picked = jnp.take(source_table, clipped, axis=1)  114 us
    unnamed x36, other arithmetic  29 us
    all_gather x1, blocking collectives, local(): group_table = lax.all_gather(top_moments, 'dev', axis=1, tiled=True)  26.8 us
    gather x26, local copies, waits for them, and re-layouts, local(): sources = jnp.take(near_table, near_lists[slot_index], axis=1)  22.9 us
    slice x26, local copies, waits for them, and re-layouts, pair_field(): weighted = sources[3][:, None, :] * inverse  20.9 us
    dot_general x3, matrix products, translate_level(): jnp.dot(operator.reshape(term_count, -1), picked.reshape(-1, source_lists...  11 us
  transfers between devices with their start and end apart: 4, of which 1 were waited for; matrix products, arithmetic and copies ran while one was open for 39% of the time, Pallas kernels for 0%

commit v1 on v0

v1 whole, which is shorter than its diff:
```python
import math

import jax
import jax.numpy as jnp
import numpy as np
from jax import lax
from jax.experimental import pallas as pl
from jax.experimental.pallas import tpu as pltpu
from jax.sharding import PartitionSpec as P

ORDER = 6
TERMS = 36
OFFS = 316
SOFTEN = 0.01
LEAVES = 128
SLOTS = 128
RANKS = 128
AXES = ("group", "dev")
F32 = jnp.float32
BF16 = jnp.bfloat16
I32 = jnp.int32
HIGH = lax.Precision.HIGHEST
VMEM = pltpu.VMEM
SMEM = pltpu.SMEM
MIB = 1 << 20
CHUNK = 4
ROWS = 64
NEAR_PAD = 28
DEPTH = 4


def harmonics(coord_x, coord_y, coord_z):
    radius_sq = coord_x * coord_x + coord_y * coord_y + coord_z * coord_z
    real_part = {(0, 0): jnp.ones_like(coord_x)}
    imag_part = {}
    for degree in range(1, ORDER):
        scale = 1.0 / (2.0 * degree)
        if degree == 1:
            real_part[1, 1] = coord_x * scale
            imag_part[1, 1] = coord_y * scale
        else:
            prior_re = real_part[degree - 1, degree - 1]
            prior_im = imag_part[degree - 1, degree - 1]
            real_part[degree, degree] = (coord_x * prior_re - coord_y * prior_im) * scale
            imag_part[degree, degree] = (coord_x * prior_im + coord_y * prior_re) * scale
        for column in range(degree):
            factor = 1.0 / ((degree + column) * (degree - column))
            lead = ((2.0 * degree - 1.0) * factor) * coord_z
            for part in (real_part, imag_part):
                if (degree - 1, column) not in part:
                    continue
                value = lead * part[degree - 1, column]
                if column <= degree - 2:
                    value = value - (radius_sq * factor) * part[degree - 2, column]
                part[degree, column] = value
    pieces = []
    for degree in range(ORDER):
        for column in range(degree + 1):
            weight = math.sqrt(math.factorial(degree - column) * math.factorial(degree + column))
            pieces.append(weight * real_part[degree, column])
            if column > 0:
                pieces.append(weight * imag_part[degree, column])
    return pieces


def near_offsets():
    shifts = []
    for step_x in (-1, 0, 1):
        for step_y in (-1, 0, 1):
            for step_z in (-1, 0, 1):
                if step_x != 0 or step_y != 0 or step_z != 0:
                    shifts.append((step_x, step_y, step_z))
    return shifts


def far_groups():
    offsets = []
    for step_x in range(-3, 4):
        for step_y in range(-3, 4):
            for step_z in range(-3, 4):
                if max(abs(step_x), abs(step_y), abs(step_z)) >= 2:
                    offsets.append((step_x, step_y, step_z))
    groups = {}
    for j, offset in enumerate(offsets):
        mask, value = 0, 0
        for axis in range(3):
            if abs(offset[axis]) == 3:
                mask |= 1 << axis
                if offset[axis] == -3:
                    value |= 1 << axis
        key = tuple(abs(v) if abs(v) == 3 else v for v in offset)
        groups.setdefault(key, []).append((j, mask, value))
    return sorted(groups.values(), key=len)


GROUPS = far_groups()


def split3(value):
    high = value.astype(BF16).astype(F32)
    rest = value - high
    mid = rest.astype(BF16).astype(F32)
    return high, mid, rest - mid


def iota(shape, dim):
    return lax.broadcasted_iota(I32, shape, dim)


def pack_kernel(send, part, cnt, tab, out):
    filled = jnp.where(iota((SLOTS, LEAVES), 0) < cnt[...], 1.0, 0.0).T
    comps = [part[0], part[1], part[2], jnp.where(filled > 0.5, part[3], 0.0)]
    for a in range(4):
        tab[pl.ds(a, LEAVES, stride=8), :] = comps[a]
        tab[pl.ds(a + 4, LEAVES, stride=8), :] = comps[a]
    upper = iota((8, 128), 0) < 4

    def body(r, carry):
        for k in range(4):
            first = jnp.maximum(send[r, 2 * k], 0)
            second = jnp.maximum(send[r, 2 * k + 1], 0)
            tile0 = tab[pl.ds(pl.multiple_of(first * 8, 8), 8), :]
            tile1 = tab[pl.ds(pl.multiple_of(second * 8, 8), 8), :]
            out[r, 8 * k : 8 * k + 8, :] = jnp.where(upper, tile0, tile1)
        return carry

    lax.fori_loop(0, RANKS, body, 0, unroll=4)


def pack_near(near_rows, particles, cnt):
    return pl.pallas_call(
        pack_kernel,
        out_shape=(
            jax.ShapeDtypeStruct((LEAVES * 8, 128), F32),
            jax.ShapeDtypeStruct((RANKS, 32, 128), F32),
        ),
        in_specs=[pl.BlockSpec(memory_space=SMEM), pl.BlockSpec(memory_space=VMEM), pl.BlockSpec(memory_space=VMEM)],
        out_specs=(pl.BlockSpec(memory_space=VMEM), pl.BlockSpec(memory_space=VMEM)),
        compiler_params=pltpu.CompilerParams(vmem_limit_bytes=32 * MIB),
        cost_estimate=pl.CostEstimate(flops=3_000_000, bytes_accessed=3 * MIB, transcendentals=0),
        name="pack_near",
    )(near_rows, particles, cnt)


def nt(left, right):
    return lax.dot_general(left, right, (((1,), (1,)), ((), ())), precision=HIGH, preferred_element_type=F32)


def moments_kernel(part, cnt, idx3, tops, upward, sent, leaf_out, mid_out, xs, table):
    filled = iota((SLOTS, LEAVES), 0) < cnt[...]
    for a in range(3):
        xs[a] = part[a].T
    xs[3] = jnp.where(filled, part[3].T, 0.0)

    def chunk(c, acc):
        rows = pl.ds(pl.multiple_of(c * 8, 8), 8)
        charge = xs[3, rows, :]
        basis = harmonics(xs[0, rows, :], xs[1, rows, :], xs[2, rows, :])
        return tuple(old + charge * value for old, value in zip(acc, basis))

    zero = jnp.zeros((8, 128), F32)
    acc = lax.fori_loop(0, SLOTS // 8, chunk, (zero,) * TERMS)
    rows = [jnp.sum(value, axis=0, keepdims=True) for value in acc]
    leaf = jnp.concatenate(rows + [jnp.zeros((4, 128), F32)], axis=0)
    leaf_out[...] = leaf
    table[...] = jnp.zeros((256, 128), F32)
    table[0:128, :] = jnp.concatenate([leaf, jnp.zeros((88, 128), F32)], axis=0).T
    mid = jnp.zeros((16, TERMS), F32)
    for o in range(8):
        mid = mid + nt(table[pl.ds(o, 16, stride=8), :][:, :TERMS], upward[o])
    table[128:144, 0:TERMS] = mid
    top = jnp.zeros((2, TERMS), F32)
    for o in range(8):
        top = top + nt(table[pl.ds(128 + o, 2, stride=8), :][:, :TERMS], upward[o])
    table[144:146, 0:TERMS] = top
    table[160:168, :] = tops[...]
    mid_wide = jnp.concatenate([table[128:144, :], jnp.zeros((112, 128), F32)], axis=0)
    mid_out[...] = mid_wide.T[0:40]
    weights = []
    for a in range(3):
        values = table[...] if a == 0 else pltpu.roll(table[...], 40 * a, 1)
        high, middle, low = split3(values)
        weights.append((jnp.concatenate([high, middle], axis=1).astype(BF16), low.astype(BF16)))
    lane = iota((128, 256), 1)

    def pick(e, carry):
        rows = pl.ds(pl.multiple_of(e * 128, 128), 128)
        columns = idx3[rows, :]
        total = jnp.zeros((128, 128), F32)
        for a in range(3):
            hot = jnp.where(columns[:, a : a + 1] == lane, 1.0, 0.0).astype(BF16)
            both = jnp.dot(hot, weights[a][0], preferred_element_type=F32)
            total = total + (both[:, :128] + both[:, 128:]) + jnp.dot(hot, weights[a][1], preferred_element_type=F32)
        sent[rows, :] = total
        return carry

    lax.fori_loop(0, 8, pick, 0)


def moments(particles, cnt, idx3, tops, upward):
    return pl.pallas_call(
        moments_kernel,
        out_shape=(
            jax.ShapeDtypeStruct((RANKS * 8, 128), F32),
            jax.ShapeDtypeStruct((40, 128), F32),
            jax.ShapeDtypeStruct((40, 128), F32),
        ),
        in_specs=[pl.BlockSpec(memory_space=VMEM)] * 5,
        out_specs=(pl.BlockSpec(memory_space=VMEM),) * 3,
        scratch_shapes=[VMEM((4, SLOTS, LEAVES), F32), VMEM((256, 128), F32)],
        compiler_params=pltpu.CompilerParams(vmem_limit_bytes=32 * MIB),
        cost_estimate=pl.CostEstimate(flops=5_000_000, bytes_accessed=2 * MIB, transcendentals=0),
        name="moments",
    )(particles, cnt, idx3, tops, upward)


def shift_tables():
    scale = np.zeros((32, 8, 128), np.float32)
    add = np.zeros((32, 8, 128), np.float32)
    shifts = near_offsets() + [(0, 0, 0)] * 6
    for j, shift in enumerate(shifts):
        for a in range(3):
            scale[j, a] = 1.0
            scale[j, a + 4] = 1.0
            add[j, a] = 2.0 * shift[a]
            add[j, a + 4] = 2.0 * shift[a]
        add[j, 3] = 1.0
    return scale.reshape(256, 128)[:8], add.reshape(256, 128)


def source_matrix(tile, scale, add, upper):
    moved = tile * scale + add
    values = jnp.where(upper, moved, moved * moved)
    high, middle, low = split3(values)
    return jnp.concatenate([high, high, middle, high, middle, low], axis=0).astype(BF16)


def near_kernel(first, lists, meta, total, tab_in, scale_in, add_in, target_in, prev, field, target_out, tab, bufs, mats, acc):
    upper = iota((8, 128), 0) < 4
    scale = scale_in[...]
    sub8 = iota((8, 128), 0)
    if first:
        n_tab = LEAVES
        tab[0 : 8 * n_tab, :] = tab_in[...]
        target = target_out

        def build(b, carry):
            tile = tab_in[pl.ds(pl.multiple_of(b * 8, 8), 8), :]
            square = jnp.where(upper & (sub8 < 3), tile * tile, 0.0)
            norm = jnp.sum(square, axis=0, keepdims=True) + SOFTEN
            values = jnp.where(sub8 < 3, -2.0 * tile, jnp.where(sub8 == 3, norm, jnp.where(sub8 < 7, 1.0, 0.0)))
            high, middle, low = split3(values)
            wide = jnp.concatenate([high, middle, high, low, middle, high], axis=0)
            target[pl.ds(pl.multiple_of(b * 128, 128), 128), :] = wide.T.astype(BF16)
            return carry

        lax.fori_loop(0, LEAVES, build, 0, unroll=2)
        target[LEAVES * 128 :, :] = jnp.zeros((128, 48), BF16)
    else:
        n_tab = RANKS * 8
        target = target_in

        def build(s, carry):
            for k in range(4):
                tile = tab_in[s, 8 * k : 8 * k + 8, :]
                turned = pltpu.roll(tile, 4, 0)
                base = pl.multiple_of(s * 64 + k * 16, 16)
                tab[pl.ds(base, 8), :] = jnp.where(upper, tile, turned)
                tab[pl.ds(base + 8, 8), :] = jnp.where(upper, turned, tile)
            return carry

        lax.fori_loop(0, RANKS, build, 0, unroll=2)
    tab[8 * n_tab : 8 * n_tab + 8, :] = jnp.zeros((8, 128), F32)

    def parts(unit):
        return unit & 255, lax.shift_right_logical(unit, 8) & 1, lax.shift_right_logical(unit, 9)

    def entry(b, ch, l):
        word = lists[ch * CHUNK + l, b]
        leaf = lax.shift_right_logical(word, 5)
        return pl.multiple_of(leaf * 8, 8), pl.multiple_of((word & 31) * 8, 8)

    def prepare(unit, mat):
        b, _, ch = parts(unit)
        for l in range(CHUNK):
            place, slot = entry(b, ch, l)
            mat[:, 128 * l : 128 * l + 128] = source_matrix(tab[pl.ds(place, 8), :], scale, add_in[pl.ds(slot, 8), :], upper)

    def distances(unit, mat, buf):
        b, rg, _ = parts(unit)
        left = target[pl.ds(pl.multiple_of(b * 128 + rg * ROWS, ROWS), ROWS), :]
        for pair in range(CHUNK // 2):
            lanes = slice(256 * pair, 256 * pair + 256)
            buf[:, lanes] = jnp.dot(left, mat[:, lanes], preferred_element_type=F32)

    def gather(unit, buf):
        b, rg, ch = parts(unit)
        part = None
        for l in range(CHUNK):
            place, _ = entry(b, ch, l)
            charge = tab[pl.ds(place, 8), :][3:4]
            term = lax.rsqrt(buf[:, 128 * l : 128 * l + 128]) * charge
            part = term if part is None else part + term
        rows = pl.ds(pl.multiple_of(b * 128 + rg * ROWS, ROWS), ROWS)
        acc[rows, :] = acc[rows, :] + part

    def following(unit):
        b, rg, ch = parts(unit)
        wrap = ch + 1 >= meta[0, b]
        ch = jnp.where(wrap, 0, ch + 1)
        rg = jnp.where(wrap, rg + 1, rg)
        done = rg >= meta[1, b]
        rg = jnp.where(done, 0, rg)
        b = jnp.minimum(jnp.where(done, b + 1, b), LEAVES)
        return b + rg * 256 + ch * 512

    if first:
        same = iota((128, 128), 0) == iota((128, 128), 1)

        def self_pairs(i, carry):
            for l in range(4):
                b = i * 4 + l
                tile = tab[pl.ds(pl.multiple_of(b * 8, 8), 8), :]
                mat = source_matrix(tile, scale, add_in[31 * 8 : 32 * 8, :], upper)
                rows = pl.ds(pl.multiple_of(b * 128, 128), 128)
                square = jnp.dot(target[rows, :], mat, preferred_element_type=F32)
                acc[rows, :] = jnp.where(same, 0.0, lax.rsqrt(square) * tile[3:4])
            return carry

        lax.fori_loop(0, LEAVES // 4, self_pairs, 0)
    else:
        acc[...] = jnp.zeros(acc.shape, F32)
    acc[LEAVES * 128 :, :] = jnp.zeros((128, 128), F32)

    def step(u, units):
        units = list(units)
        for n in range(DEPTH):
            gather(units[n], bufs.at[n])
        for n in range(DEPTH):
            distances(units[DEPTH + n], mats.at[n], bufs.at[n])
        for n in range(DEPTH):
            prepare(units[2 * DEPTH + n], mats.at[n])
        for n in range(DEPTH):
            units.append(following(units[-1]))
        return tuple(units[DEPTH:])

    units = [jnp.int32(LEAVES)] * (2 * DEPTH) + [jnp.int32(0)]
    for n in range(DEPTH - 1):
        units.append(following(units[-1]))
    lax.fori_loop(0, (total[0] + (DEPTH - 1)) // DEPTH + 2, step, tuple(units))

    field[...] = jnp.zeros((128, 128), F32) if prev is None else prev[...]
    lane = iota((128, 128), 1)

    def reduce(i, carry):
        value = field[...]
        for l in range(8):
            b = i * 8 + l
            rows = pl.ds(pl.multiple_of(b * 128, 128), 128)
            value = jnp.where(lane == b, value + jnp.sum(acc[rows, :], axis=1, keepdims=True), value)
        field[...] = value
        return carry

    lax.fori_loop(0, LEAVES // 8, reduce, 0)


def near_pass(lists, meta, total, tab, target=None, prev=None):
    first = target is None
    scale, add = shift_tables()
    n_tab = LEAVES if first else RANKS * 8
    v = pl.BlockSpec(memory_space=VMEM)
    s = pl.BlockSpec(memory_space=SMEM)
    scratch = [
        VMEM((8 * n_tab + 8, 128), F32),
        VMEM((DEPTH, ROWS, 128 * CHUNK), F32),
        VMEM((DEPTH, 48, 128 * CHUNK), BF16),
        VMEM(((LEAVES + 1) * 128, 128), F32),
    ]
    params = pltpu.CompilerParams(vmem_limit_bytes=48 * MIB)
    cost = pl.CostEstimate(flops=30_000_000_000, bytes_accessed=8 * MIB, transcendentals=20_000_000)
    field_type = jax.ShapeDtypeStruct((128, 128), F32)
    if first:

        def kernel(lists, meta, total, tab_in, scale_in, add_in, field, target_out, *rest):
            near_kernel(True, lists, meta, total, tab_in, scale_in, add_in, None, None, field, target_out, *rest)

        return pl.pallas_call(
            kernel,
            out_shape=(field_type, jax.ShapeDtypeStruct(((LEAVES + 1) * 128, 48), BF16)),
            in_specs=[s, s, s, v, v, v],
            out_specs=(v, v),
            scratch_shapes=scratch,
            compiler_params=params,
            cost_estimate=cost,
            name="near_own",
        )(lists, meta, total, tab, jnp.asarray(scale), jnp.asarray(add))

    def kernel(lists, meta, total, tab_in, scale_in, add_in, target_in, prev, field, *rest):
        near_kernel(False, lists, meta, total, tab_in, scale_in, add_in, target_in, prev, field, None, *rest)

    return pl.pallas_call(
        kernel,
        out_shape=field_type,
        in_specs=[s, s, s, v, v, v, v, v],
        out_specs=v,
        scratch_shapes=scratch,
        compiler_params=params,
        cost_estimate=cost,
        name="near_received",
    )(lists, meta, total, tab, jnp.asarray(scale), jnp.asarray(add), target, prev)


def near_tables(near_lists, counts):
    own = near_lists < LEAVES
    before = jnp.cumsum(own.astype(I32), axis=0)
    order = jnp.arange(1, 27, dtype=I32)[:, None]
    slot = jnp.arange(26, dtype=I32)[:, None]
    groups = (counts + (ROWS - 1)) // ROWS
    result = []
    for mine, place, base, dummy in ((own, before - 1, 0, LEAVES), (~own, order - before - 1, LEAVES, RANKS * 8)):
        word = (near_lists - base) * 32 + slot - dummy * 32
        place = jnp.where(mine, place, -1)
        hits = place[None] == jnp.arange(NEAR_PAD, dtype=I32)[:, None, None]
        table = jnp.sum(jnp.where(hits, word[None], 0), axis=1) + dummy * 32
        table = jnp.pad(table, ((0, 0), (0, 8)), constant_values=dummy * 32)
        number = jnp.sum(mine.astype(I32), axis=0)
        chunks = jnp.maximum((number + (CHUNK - 1)) // CHUNK, 1)
        meta = jnp.pad(jnp.stack([chunks, groups]), ((0, 0), (0, 8)), constant_values=1)
        result.append((table, meta, jnp.sum(chunks * groups).reshape(1)))
    return result


def group_table():
    rows = []
    for group in GROUPS:
        rows.append([word for entry in group for word in entry])
    return rows


N1 = sum(len(g) == 1 for g in GROUPS)
N2 = sum(len(g) == 2 for g in GROUPS)
N4 = sum(len(g) == 4 for g in GROUPS)
N8 = sum(len(g) == 8 for g in GROUPS)
MERGED = len(GROUPS)
MERGED_PAD = 192


def group_words():
    words = np.zeros((MERGED_PAD, 8), np.int32)
    for m, group in enumerate(GROUPS):
        for g in range(8):
            j, mask, value = group[min(g, len(group) - 1)]
            words[m, g] = j * 64 + mask * 8 + value
    return words


def far_kernel(
    words, where_am_i, recv, leaf, mid, far_lists, small_lists, operators, downward, part, cnt, near,
    out, rt, merged, wide, small, xs, parents, leaves,
):
    for i in range(8):
        rt[:, 128 * i : 128 * i + 128] = recv[128 * i : 128 * i + 128, :].T

    def two(value):
        high = value.astype(BF16).astype(F32)
        return jnp.concatenate([high, value - high], axis=0).astype(BF16)

    table = two(jnp.concatenate([leaf[...], rt[0:40, :], rt[40:80, :]], axis=1))
    for m, group in enumerate(GROUPS):
        row = far_lists[group[0][0] : group[0][0] + 1, :]
        for j, _, _ in group[1:]:
            row = jnp.maximum(row, far_lists[j : j + 1, :])
        merged[m : m + 1, :] = row
    merged[MERGED:, :] = jnp.full((MERGED_PAD - MERGED, 128), -1, I32)
    index = merged[...]
    rel = index - LEAVES
    slot = rel & 15
    moved = LEAVES + lax.shift_right_logical(slot, 3) * 1024 + lax.shift_right_logical(rel, 4) * 8 + (slot & 7)
    merged[...] = jnp.where(rel >= 0, moved, index)
    lane = iota((40, 128), 1)

    def hot(row, depth):
        width = row.shape[1]
        upper = lax.shift_right_arithmetic(row, 8)
        lower = (row & 255).astype(F32)
        pieces = []
        for c in range((depth + 255) // 256):
            height = min(256, depth - 256 * c)
            target = jnp.where(upper == c, lower, -1.0)
            number = iota((height, width), 0).astype(F32)
            pieces.append(jnp.where(target == number, 1.0, 0.0).astype(BF16))
        return jnp.concatenate(pieces, axis=0)

    def expand(values, m, size):
        for g in range(size):
            word = words[m, g]
            j = lax.shift_right_logical(word, 6)
            keep = (lane & (lax.shift_right_logical(word, 3) & 7)) == (word & 7)
            wide[pl.ds(j, 40, stride=320), :] = jnp.where(keep, values, 0.0)

    def block(first_row, size):
        def body(i, carry):
            m = first_row + 2 * i
            row = jnp.concatenate([merged[pl.ds(m, 1), :], merged[pl.ds(m + 1, 1), :]], axis=1)
            both = jnp.dot(table, hot(row, 2176), preferred_element_type=F32)
            value = both[0:40] + both[40:80]
            expand(value[:, :128], m, size)
            expand(value[:, 128:], m + 1, size)
            return carry

        return body

    lax.fori_loop(0, N1 // 2, block(0, 1), 0)
    lax.fori_loop(0, (N2 + 1) // 2, block(N1, 2), 0)
    lax.fori_loop(0, (N4 + N8) // 2, block(N1 + N2, 8), 0)

    def contract(left, right, dims):
        lh = left.astype(BF16)
        ll = (left - lh.astype(F32)).astype(BF16)
        rh = right.astype(BF16)
        rl = (right - rh.astype(F32)).astype(BF16)
        dot = lambda a, b: lax.dot_general(a, b, (dims, ((), ())), preferred_element_type=F32)
        return dot(lh, rh) + dot(ll, rh) + dot(lh, rl)

    local = jnp.zeros((TERMS, 128), F32)
    for k in range(TERMS):
        local = local + contract(operators[0, :, k, :], wide[320 * k : 320 * k + OFFS, :], ((1,), (0,)))

    table_small = two(jnp.concatenate([mid[...], rt[80:120, :]], axis=1))
    lists = small_lists[...]
    rel = lists - 16
    mid_place = jnp.where(rel >= 0, LEAVES + lax.shift_right_logical(rel, 2) * 8 + (rel & 3), lists)
    me = where_am_i[0]
    group = lax.shift_right_logical(me, 5)
    top_place = jnp.where(lists >= 0, LEAVES + (group * 32 + lax.shift_right_arithmetic(lists, 1)) * 8 + 4 + (lists & 1), -1)
    for h in range(4):
        row = recv[pl.ds((h * 32 + (me & 31)) * 8 + 6, 1), :]
        for c in range(4):
            box = row[:, 120 + c : 121 + c].astype(I32)
            place = LEAVES + (h * 32 + lax.shift_right_arithmetic(box, 1)) * 8 + 4 + (box & 1)
            top_place = jnp.where(lists == 64 + 4 * h + c, place, top_place)
    place = jnp.where(iota(lists.shape, 0) < 16, mid_place, top_place)
    for t in range(18):
        both = jnp.dot(table_small, hot(place[t : t + 1], 1152), preferred_element_type=F32)
        value = both[0:40] + both[40:80]
        for c in range(3):
            small[c, 40 * t : 40 * t + 40, :] = value[:, 128 * c : 128 * c + 128]
    mid_local = jnp.zeros((16, TERMS), F32)
    top_local = jnp.zeros((2, TERMS), F32)

    def every_40th(start, size):
        return jnp.concatenate([small[c, pl.ds(start, size, stride=40), :] for c in range(3)], axis=1)[:, :OFFS]

    for k in range(TERMS):
        dims = ((1,), (1,))
        mid_local = mid_local + contract(every_40th(k, 16), operators[1, :, k, :], dims)
        top_local = top_local + contract(every_40th(640 + k, 2), operators[2, :, k, :], dims)

    for o in range(8):
        parents[pl.ds(o, 2, stride=8), 0:TERMS] = nt(top_local, downward[o])
    mid_total = parents[:, 0:TERMS] + mid_local
    leaves[...] = jnp.zeros((128, 128), F32)
    for o in range(8):
        leaves[pl.ds(o, 16, stride=8), 0:TERMS] = nt(mid_total, downward[o])
    leaves[...] = leaves[...].T
    leaves[0:TERMS, :] = leaves[0:TERMS, :] + local
    for a in range(3):
        xs[a] = part[a].T

    def chunk(c, carry):
        rows = pl.ds(pl.multiple_of(c * 8, 8), 8)
        basis = harmonics(xs[0, rows, :], xs[1, rows, :], xs[2, rows, :])
        total = near[rows, :]
        for k in range(TERMS):
            total = total + leaves[k : k + 1, :] * basis[k]
        xs[3, rows, :] = jnp.where(iota((8, 128), 0) + c * 8 < cnt[...], total, 0.0)
        return carry

    lax.fori_loop(0, SLOTS // 8, chunk, 0)
    out[...] = xs[3].T


def far_pass(where_am_i, recv, leaf, mid, far_lists, small_lists, translate, downward, particles, cnt, near):
    v = pl.BlockSpec(memory_space=VMEM)
    s = pl.BlockSpec(memory_space=SMEM)
    return pl.pallas_call(
        far_kernel,
        out_shape=jax.ShapeDtypeStruct((LEAVES, SLOTS), F32),
        in_specs=[s, s] + [v] * 10,
        out_specs=v,
        scratch_shapes=[
            VMEM((128, 1024), F32),
            VMEM((MERGED_PAD, 128), I32),
            VMEM((40 * 320, 128), F32),
            VMEM((3, 18 * 40, 128), F32),
            VMEM((4, 128, 128), F32),
            VMEM((16, 128), F32),
            VMEM((128, 128), F32),
        ],
        compiler_params=pltpu.CompilerParams(vmem_limit_bytes=48 * MIB),
        cost_estimate=pl.CostEstimate(flops=20_000_000_000, bytes_accessed=10 * MIB, transcendentals=0),
        name="far_pass",
    )(jnp.asarray(group_words()), where_am_i, recv, leaf, mid, far_lists, small_lists, translate, downward, particles, cnt, near)


def local(
    particles,
    counts,
    upward,
    downward,
    translate,
    far_send,
    mid_send,
    top_send,
    near_send,
    far_lists,
    mid_lists,
    top_lists,
    near_lists,
):
    me = lax.axis_index("group") * 32 + lax.axis_index("dev")
    cnt = counts.reshape(1, LEAVES)
    tab, near_out = pack_near(near_send[0], particles, cnt)
    near_in = lax.all_to_all(near_out, AXES, split_axis=0, concat_axis=0, tiled=True)

    far_rows = far_send[0]
    mid_rows = jnp.where(mid_send[0] >= 0, mid_send[0] + 128, -1)
    rank = jnp.arange(RANKS, dtype=I32)[:, None]
    tail = jnp.concatenate([jnp.full((RANKS, 1), 144, I32), jnp.full((RANKS, 1), 145, I32), 160 + rank // 32, jnp.full((RANKS, 1), -1, I32)], axis=1)
    idx3 = jnp.stack([far_rows[:, :8], far_rows[:, 8:], jnp.concatenate([mid_rows, tail], axis=1)], axis=-1)
    tops = jnp.pad(top_send[0].astype(F32), ((0, 4), (40, 84)))
    sent, leaf, mid = moments(particles, cnt, idx3.reshape(RANKS * 8, 3), tops, upward)
    recv = lax.all_to_all(sent.reshape(RANKS, 8, 128), AXES, split_axis=0, concat_axis=0, tiled=True)

    own, received = near_tables(near_lists, counts)
    near, target = near_pass(*own, tab)
    near = near_pass(*received, near_in, target, near)
    small_lists = jnp.pad(jnp.concatenate([mid_lists, top_lists], axis=1).T, ((0, 6), (0, 68)), constant_values=-1)
    return far_pass(
        me.reshape(1), recv.reshape(RANKS * 8, 128), leaf, mid, far_lists, small_lists, translate, downward, particles, cnt, near
    )


def solution(mesh):
    in_specs = (
        P(None, AXES, None),
        P(AXES),
        P(),
        P(),
        P(),
        P(AXES, None, None),
        P(AXES, None, None),
        P(AXES, None, None),
        P(AXES, None, None),
        P(None, AXES),
        P(None, AXES),
        P(None, AXES),
        P(None, AXES),
    )
    return jax.shard_map(local, mesh=mesh, in_specs=in_specs, out_specs=P(AXES, None), check_vma=False)
```

time: 537 us -> 232 us (0.43); the launches traced: 527 us -> 231 us
  other arithmetic: 239 us -> 1.08 us
  local copies, waits for them, and re-layouts: 204 us -> 10.4 us
  Pallas kernels: 0 us -> 192 us
  blocking collectives: 26.8 us -> 0 us
  matrix products: 21.3 us -> 0 us
    pallas_call x0 -> x5, Pallas kernels: none -> 192 us  [the longest x1 83.5 us: near_pass(): pl.pallas_call(kernel, out_shape=(field_type, jax.ShapeDtypeStruct(((LEAV...]
    reduce_sum x7 -> x3, other arithmetic: 168 us -> 0.88 us  [the longest x1 0.73 us: near_tables(): result.append((table, meta, jnp.sum(chunks * groups).reshape(1)))]
    gather x36 -> x0, local copies, waits for them, and re-layouts: 152 us -> none  [the longest x6 114 us: translate_level(): picked = jnp.take(source_table, clipped, axis=1)]
    unnamed x36 -> x0, other arithmetic: 29 us -> none
    all_gather x1 -> x0, blocking collectives: 26.8 us -> none  [local(): group_table = lax.all_gather(top_moments, 'dev', axis=1, tiled=True)]
    slice x29 -> x3, local copies, waits for them, and re-layouts: 26.8 us -> 0.21 us  [the longest x2 0.1 us: local(): far_rows[:, :8]]
    select_n x32 -> x2, other arithmetic: 23.5 us -> 0.08 us  [the longest x1 0.08 us: near_tables(): place = jnp.where(mine, place, -1)]
    dot_general x9 -> x0, matrix products: 21.3 us -> none  [the longest x3 11 us: translate_level(): jnp.dot(operator.reshape(term_count, -1), picked.reshape(-1, source_lists...]
  transfers between devices with their start and end apart: 4 -> 2, of which waited for: 1 -> 0; matrix products, arithmetic and copies ran while one was open for 39% -> 1% of each run, Pallas kernels for 0% -> 53%
where the time goes in v1:
time: 232 us; the launch traced here: 231 us
  Pallas kernels  192 us (83%)
  starting transfers between devices  26.4 us (11%)
  local copies, waits for them, and re-layouts  10.4 us (4%)
    pallas_call x1, Pallas kernels, near_pass(): pl.pallas_call(kernel, out_shape=(field_type, jax.ShapeDtypeStruct(((LEAV...  83.5 us
    pallas_call x1, Pallas kernels, far_pass(): pl.pallas_call(far_kernel, out_shape=jax.ShapeDtypeStruct((LEAVES, SLOTS)...  66.8 us
    pallas_call x1, Pallas kernels, near_pass(): pl.pallas_call(kernel, out_shape=field_type, in_specs=[s, s, s, v, v, v,...  32.9 us
    all_to_all x1, starting transfers between devices, local(): lax.all_to_all(sent.reshape(RANKS, 8, 128), AXES, split_axis=0, concat_ax...  14.9 us
    all_to_all x1, starting transfers between devices, local(): lax.all_to_all(near_out, AXES, split_axis=0, concat_axis=0, tiled=True)  11.5 us
    unnamed x47, local copies, waits for them, and re-layouts  9.43 us
    pallas_call x1, Pallas kernels, moments(): pl.pallas_call(moments_kernel, out_shape=(jax.ShapeDtypeStruct((RANKS * 8...  5.7 us
  transfers between devices with their start and end apart: 2, of which 0 were waited for; matrix products, arithmetic and copies ran while one was open for 1% of the time, Pallas kernels for 53%

profile of v1, /device:TPU:1, one launch (start us, length us, event | category | flops | bytes accessed | tf_op | source)
XLA Modules:
  0.0 230.6 jit_solution(2740489559271481401)
XLA Ops:
  0.0 0.0 copy-start.20
  0.1 0.9 copy.46
  0.9 0.9 copy-done.1
  1.9 0.7 copy-done.3
  2.5 3.5 %pack_near.1 = (f32[1024,128]{1,0:T(8,128)S(1)}, f32[128,32,128]{2,1,0:T(8,128)S(1)}) custom-call(s32[128,8]{1,0:T(8,128)S(1)} %bitcast.36, f32[4,128,128]{2,1,0:T(8,128)S(1)} %copy-done.1, s32[1,128]{1,0:T(1,128)S(1)} %bitcast.37), custom_call_target="tpu_custom_call" | custom-call | flops 3000000 | bytes 3145728 | tf_op jit(solution)/shard_map/pack_near/pallas_call | solution.py:131
  6.0 1.3 copy-done
  7.4 0.8 copy-done.5
  8.1 11.5 %all-to-all-start.1 = ((f32[128,32,128]{2,1,0:T(8,128)}), f32[128,32,128]{2,1,0:T(8,128)S(1)}, u32[]{:S(2)}, u32[]{:S(2)}) async-start(f32[128,32,128]{2,1,0:T(8,128)} %copy-done), calls=%async_computation.1 | async-start | bytes 4194304 | tf_op jit(solution)/shard_map/all_to_all | solution.py:624
  19.7 0.7 multiply_reduce_fusion
  20.6 0.1 add_select_fusion
  20.7 0.1 select_reduce_fusion
  20.8 0.1 copy.41
  20.9 0.1 stack.24
  21.1 0.1 copy.43
  21.2 0.1 stack.26
  21.3 0.1 copy.42
  21.4 0.1 stack.25
  21.7 0.2 copy.44.idx3
  21.9 0.1 pad.22.tops
  22.0 5.7 %moments.1 = (f32[1024,128]{1,0:T(8,128)}, f32[40,128]{1,0:T(8,128)S(1)}, f32[40,128]{1,0:T(8,128)S(1)}) custom-call(f32[4,128,128]{2,1,0:T(8,128)S(1)} %copy-done.2, s32[1,128]{1,0:T(1,128)S(1)} %bitcast.38, s32[1024,3]{1,0:T(8,128)S(1)} %copy.44.idx3, f32[8,128]{1,0:T(8,128)S(1)} %pad.22.tops, f32[8,36,36]{2,1,0:T(8,128)S(1)} %copy.45.upward), custom_call_target="tpu_custom_call" | custom-call | flops 5000000 | bytes 2097152 | tf_op jit(solution)/shard_map/moments/pallas_call | solution.py:201
  27.7 1.0 copy-done.6
  28.8 83.5 %near_own.1 = (f32[128,128]{1,0:T(8,128)S(1)}, bf16[16512,48]{1,0:T(8,128)(2,1)S(1)}) custom-call(s32[28,136]{1,0:T(8,128)S(1)} %pad.26.lists, s32[2,136]{1,0:T(2,128)S(1)} %pad.27.meta, s32[1]{0:T(128)} %bitcast.13.total, f32[1024,128]{1,0:T(8,128)S(1)} %copy-done.6, f32[8,128]{1,0:T(8,128)S(1)} %copy-done.10, f32[256,128]{1,0:T(8,128)S(1)} %copy-done.8), custom_call_target="tpu_custom_call" | custom-call | flops 30000001024 | bytes 8388608 | tf_op jit(solution)/shard_map/near_own/pallas_call | solution.py:387
  112.3 2.0 copy-done.11
  114.2 0.0 all-to-all-done.1.tab_in
  114.2 14.9 %all-to-all-start = ((f32[128,8,128]{2,1,0:T(8,128)}), f32[128,8,128]{2,1,0:T(8,128)S(1)}, u32[]{:S(2)}, u32[]{:S(2)}) async-start(f32[128,8,128]{2,1,0:T(8,128)} %bitcast.5), calls=%async_computation | async-start | bytes 1048576 | tf_op jit(solution)/shard_map/all_to_all | solution.py:633
  129.1 0.0 copy-start.13
  129.2 0.8 copy-done.13
  130.0 32.9 %near_received.1.near = f32[128,128]{1,0:T(8,128)S(1)} custom-call(s32[28,136]{1,0:T(8,128)S(1)} %pad.24.lists, s32[2,136]{1,0:T(2,128)S(1)} %pad.25.meta, s32[1]{0:T(128)} %bitcast.10.total, f32[128,32,128]{2,1,0:T(8,128)S(1)} %all-to-all-done.1.tab_in, f32[8,128]{1,0:T(8,128)S(1)} %copy-done.10, f32[256,128]{1,0:T(8,128)S(1)} %copy-done.8, ...), custom_call_target="tpu_custom_call" | custom-call | flops 30000001024 | bytes 8388608 | tf_op jit(solution)/shard_map/near_received/pallas_call | solution.py:401
  162.9 0.0 all-to-all-done
  162.9 0.0 copy-start.9
  162.9 0.9 copy-done.9
  163.8 66.8 %far_pass.1 = f32[128,128]{1,0:T(8,128)} custom-call(s32[192,8]{1,0:T(8,128)S(1)} %copy-done.9, s32[1]{0:T(128)} %bitcast.where_am_i, f32[1024,128]{1,0:T(8,128)S(1)} %bitcast.35, f32[40,128]{1,0:T(8,128)S(1)} %get-tuple-element.13.leaf, f32[40,128]{1,0:T(8,128)S(1)} %get-tuple-element.14.mid, s32[316,128]{1,0:T(8,128)S(1)} %copy-done.7, ...), custom_call_target="tpu_custom_call" | custom-call | flops 20000000000 | bytes 10485760 | tf_op jit(solution)/shard_map/far_pass/pallas_call | solution.py:586
  (58 shorter events, 0.3 us)
Async XLA Ops:
  0.0 27.7 %copy-start.10 = (f32[8,128]{1,0:T(8,128)S(1)}, f32[8,128]{1,0:T(8,128)}, u32[]{:S(2)}) copy-start(f32[8,128]{1,0:T(8,128)} %constant.106.clone.scale_in) | copy-start | bytes 12292
  0.0 22.0 %copy-start.4 = (s32[128]{0:T(128)S(1)}, s32[128]{0:T(128)}, u32[]{:S(2)}) copy-start(s32[128]{0:T(128)} %param.19) | copy-start | bytes 1540
  0.0 19.7 %copy-start.17 = (s32[26,128]{1,0:T(8,128)S(1)}, s32[26,128]{1,0:T(8,128)}, u32[]{:S(2)}) copy-start(s32[26,128]{1,0:T(8,128)} %param.30) | copy-start | bytes 39940
  0.0 20.5 %copy-start.20 = (s32[1,128,4]{1,2,0:T(4,128)S(1)}, s32[1,128,4]{1,2,0:T(4,128)}, u32[]{:S(2)}) copy-start(s32[1,128,4]{1,2,0:T(4,128)} %param.24) | copy-start | bytes 6148
  0.0 20.5 %copy-start.21 = (s32[1,4,4]{2,1,0:T(4,128)S(1)}, s32[1,4,4]{2,1,0:T(4,128)}, u32[]{:S(2)}) copy-start(s32[1,4,4]{2,1,0:T(4,128)} %param.25) | copy-start | bytes 196
  0.0 20.5 %copy-start.18 = (s32[1,128,16]{1,2,0:T(8,128)S(1)}, s32[1,128,16]{1,2,0:T(8,128)}, u32[]{:S(2)}) copy-start(s32[1,128,16]{1,2,0:T(8,128)} %param.23) | copy-start | bytes 24580
  0.0 21.0 %copy-start.19 = (s32[316,2]{0,1:T(2,128)S(1)}, s32[316,2]{0,1:T(2,128)}, u32[]{:S(2)}) copy-start(s32[316,2]{0,1:T(2,128)} %param.29) | copy-start | bytes 7588
  0.0 21.0 %copy-start.16 = (s32[316,16]{0,1:T(8,128)S(1)}, s32[316,16]{0,1:T(8,128)}, u32[]{:S(2)}) copy-start(s32[316,16]{0,1:T(8,128)} %param.28) | copy-start | bytes 60676
  0.9 0.9 copy-start.1
  1.9 0.7 copy-start.3
  2.5 19.0 %copy-start.14 = (f32[8,36,36]{2,0,1:T(8,128)S(1)}, f32[8,36,36]{2,0,1:T(8,128)}, u32[]{:S(2)}) copy-start(f32[8,36,36]{2,0,1:T(8,128)} %param.20) | copy-start | bytes 124420
  2.5 19.1 %copy-start.15 = (f32[8,36,36]{2,0,1:T(8,128)S(1)}, f32[8,36,36]{2,0,1:T(8,128)}, u32[]{:S(2)}) copy-start(f32[8,36,36]{2,0,1:T(8,128)} %param.21) | copy-start | bytes 124420
  2.5 19.5 %copy-start.2 = (f32[4,128,128]{2,1,0:T(8,128)S(1)}, f32[4,128,128]{2,1,0:T(8,128)}, u32[]{:S(2)}) copy-start(f32[4,128,128]{2,1,0:T(8,128)} %part.5) | copy-start | bytes 786436
  2.5 25.2 %copy-start.8 = (f32[256,128]{1,0:T(8,128)S(1)}, f32[256,128]{1,0:T(8,128)}, u32[]{:S(2)}) copy-start(f32[256,128]{1,0:T(8,128)} %constant.107.clone.add_in) | copy-start | bytes 393220
  6.0 1.4 copy-start
  7.4 0.8 copy-start.5
  8.1 106.1 %all-to-all-start.1 = ((f32[128,32,128]{2,1,0:T(8,128)}), f32[128,32,128]{2,1,0:T(8,128)S(1)}, u32[]{:S(2)}, u32[]{:S(2)}) async-start(f32[128,32,128]{2,1,0:T(8,128)} %copy-done), calls=%async_computation.1 | async-start | bytes 4194304 | tf_op jit(solution)/shard_map/all_to_all | solution.py:624
  27.7 1.0 copy-start.6
  112.3 2.0 copy-start.11
  114.2 14.9 %copy-start.12 = (f32[128,128]{1,0:T(8,128)}, f32[128,128]{1,0:T(8,128)S(1)}, u32[]{:S(2)}) copy-start(f32[128,128]{1,0:T(8,128)S(1)} %get-tuple-element.18.prev) | copy-start | bytes 196612
  114.2 48.7 %all-to-all-start = ((f32[128,8,128]{2,1,0:T(8,128)}), f32[128,8,128]{2,1,0:T(8,128)S(1)}, u32[]{:S(2)}, u32[]{:S(2)}) async-start(f32[128,8,128]{2,1,0:T(8,128)} %bitcast.5), calls=%async_computation | async-start | bytes 1048576 | tf_op jit(solution)/shard_map/all_to_all | solution.py:633
  129.1 0.8 copy-start.13
  130.0 32.9 %copy-start.7 = (s32[316,128]{1,0:T(8,128)S(1)}, s32[316,128]{1,0:T(8,128)}, u32[]{:S(2)}) copy-start(s32[316,128]{1,0:T(8,128)} %far_lists.1) | copy-start | bytes 485380
  162.9 0.9 copy-start.9
